TPU v7x, 1024 devices: a whole 4x4x32 slice. The times are simulated.
1024 devices in a mesh: dp: 16 (over z_lo), node: 4 (over z_hi, core), innode: 16 (over y, x).
Axes of the slice: x: 4, y: 4, z: 32 (z_hi: 2, z_lo: 16; z = z_hi * 16 + z_lo), core: 2. Of those that a mesh axis runs over, the one named last changes fastest.
Arguments:
- tokens: bfloat16 [64, 16, 4096], P(('node', 'innode'), 'dp'), may hold values from -6 to 6
- routes: int32 [64, 16, 8], P(('node', 'innode'), 'dp'), may hold values from 0 to 63, all different within a row; in each aligned block of 16 rows (0 to 15, 16 to 31, ..., all dimensions but the last counted through in order) at most 4 rows name the same one
- gate_num: int32 [64, 16, 8], P(('node', 'innode'), 'dp'), may hold values from 16 to 128
- w_gate: bfloat16 [64, 4096, 2048], P(('node', 'innode'), None, 'dp'), may hold values from -0.09375 to 0.09375
- w_up: bfloat16 [64, 4096, 2048], P(('node', 'innode'), None, 'dp'), may hold values from -0.09375 to 0.09375
- w_down: bfloat16 [64, 2048, 4096], P(('node', 'innode'), 'dp'), may hold values from -0.125 to 0.125
Outputs:
- combined: bfloat16 [64, 16, 4096], P(('node', 'innode'), 'dp')
- expert_load: float32 [64], replicated
- balance_loss: float32 [], replicated
Inputs may be any that keep to these rules, and one draw needn't show every extreme that they name: `routes`: each token names 8 different experts and every expert is named somewhere. Within each aligned block of 16 tokens (one column, one index of node and innode) no expert is named by more than 4 tokens, and in some blocks some expert is named by exactly 4. `gate_num`: gate weight numerators over 256.
All inputs are finite; a program needn't handle non-finite values.
Results may differ from a plain program's by a relative error of at most 0.008.
Values may be sent and summed in bfloat16 or wider, within the bound.
A program may use at most 32 MiB of HBM per device.

v0:
```python
import jax
import jax.numpy as jnp
from jax import lax
from jax.sharding import PartitionSpec as P

GATE_DEN = 256


def apply_experts(grouped, w_gate, w_up, w_down):
    gate_proj = jnp.einsum("sekd,edh->sekh", grouped, w_gate, preferred_element_type=jnp.float32)
    up_proj = jnp.einsum("sekd,edh->sekh", grouped, w_up, preferred_element_type=jnp.float32)
    hidden = (jax.nn.silu(gate_proj) * up_proj).astype(jnp.bfloat16)
    return jnp.einsum("sekh,ehd->sekd", hidden, w_down, preferred_element_type=jnp.float32).astype(
        jnp.bfloat16
    )


def exclusive_ranks(onehot):
    before = jnp.cumsum(onehot, axis=0) - onehot
    return jnp.sum(before * onehot, axis=1)


def shards(tokens, routes, gate_num, w_gate, w_up, w_down):
    local_experts = w_gate.shape[0]
    node_count = lax.axis_size("node")
    experts_all = node_count * lax.axis_size("innode") * local_experts
    features = tokens.shape[2]
    own_routes = routes[0]
    per_token = own_routes.shape[1]
    own_numer = gate_num[0].astype(jnp.float32)
    shares = own_numer / jnp.sum(own_numer, axis=1, keepdims=True)
    matches = (
        own_routes[:, :, None] == jnp.arange(experts_all, dtype=jnp.int32)[None, None, :]
    ).astype(jnp.float32)
    counts = jnp.sum(matches, axis=(0, 1))
    share_sums = jnp.einsum("tk,tke->e", shares, matches)
    counts, share_sums = lax.psum((counts, share_sums), ("dp", "node", "innode"))
    total_tokens = lax.axis_size("dp") * node_count * lax.axis_size("innode") * own_routes.shape[0]
    expert_load = counts * (experts_all / (per_token * total_tokens))
    mean_share = share_sums / total_tokens
    balance_loss = jnp.sum(expert_load * mean_share)
    column_x, column_r, column_g = (
        lax.all_gather(tokens, "dp", axis=1, tiled=True),
        lax.all_gather(routes, "dp", axis=1, tiled=True),
        lax.all_gather(gate_num, "dp", axis=1, tiled=True),
    )
    column_x = column_x[0]
    column_r = column_r[0]
    column_g = column_g[0]
    col_count = column_r.shape[0]
    capacity = min(col_count, 2 * col_count * per_token // experts_all)
    flat_routes = column_r.reshape(-1)
    onehot = (flat_routes[:, None] == jnp.arange(experts_all, dtype=jnp.int32)[None, :]).astype(
        jnp.int32
    )
    slot_index = flat_routes * capacity + exclusive_ranks(onehot)
    source_row = jnp.arange(flat_routes.shape[0], dtype=jnp.int32) // per_token
    outgoing = (
        jnp.zeros((experts_all * capacity, features), jnp.bfloat16)
        .at[slot_index]
        .set(column_x[source_row])
    )
    received = lax.all_to_all(
        outgoing.reshape(experts_all, capacity, features),
        ("node", "innode"),
        split_axis=0,
        concat_axis=0,
        tiled=True,
    )
    sources = received.shape[0] // local_experts
    slots_taken = received.shape[1]
    grouped = received.reshape(sources, local_experts, slots_taken, features)
    outputs = apply_experts(grouped, w_gate, w_up, w_down)
    outputs = outputs.reshape(sources * local_experts, slots_taken, features)
    returned = lax.all_to_all(outputs, ("node", "innode"), split_axis=0, concat_axis=0, tiled=True)
    picked = returned.reshape(experts_all * capacity, features)[slot_index]
    weights = (column_g.astype(jnp.float32) / GATE_DEN).astype(jnp.bfloat16)
    partial_value = jnp.einsum(
        "tk,tkd->td",
        weights,
        picked.reshape(col_count, per_token, features),
        preferred_element_type=jnp.float32,
    )
    combined = lax.psum_scatter(partial_value[None], "dp", scatter_dimension=1, tiled=True).astype(
        jnp.bfloat16
    )
    return (combined, expert_load, balance_loss)


def solution(mesh):
    in_specs = (
        P(("node", "innode"), "dp", None),
        P(("node", "innode"), "dp", None),
        P(("node", "innode"), "dp", None),
        P(("node", "innode"), None, "dp"),
        P(("node", "innode"), None, "dp"),
        P(("node", "innode"), "dp", None),
    )
    out_specs = (P(("node", "innode"), "dp", None), P(), P())
    return jax.shard_map(shards, mesh=mesh, in_specs=in_specs, out_specs=out_specs, check_vma=False)
```

profile of v0, /device:TPU:1, one launch (start us, length us, event | category | flops | bytes accessed | tf_op | source)
XLA Modules:
  0.0 969.1 jit_solution(5953846522783169233)
XLA Ops:
  0.6 0.0 copy-start
  0.7 104.1 %all_gather.10 = s32[1,16,8]{2,0,1:T(1,128)S(1)} all-gather(s32[1,1,8]{2,0,1:T(1,128)} %bitcast.82), channel_id=1, replica_groups=mesh['dp'=16,'node'=4,'innode'=16] {'dp'}, dimensions={1}, use_global_device_ids=true | all-gather | bytes 544 | tf_op jit(solution)/shard_map/all_gather | solution.py:44
  104.8 0.5 broadcast.166
  105.3 0.7 fusion.47
  106.0 0.1 eq.61
  106.1 0.1 fusion.37
  106.2 0.2 reduce_window_sum.11
  106.4 0.2 select_reduce_fusion
  106.5 0.1 mul.37
  106.6 82.0 %all_gather.11 = bf16[1,16,4096]{2,0,1:T(2,128)(2,1)S(1)} all-gather(bf16[1,1,4096]{2,0,1:T(2,128)(2,1)} %bitcast.80), channel_id=1, replica_groups=mesh['dp'=16,'node'=4,'innode'=16] {'dp'}, dimensions={1}, use_global_device_ids=true | all-gather | bytes 139264 | tf_op jit(solution)/shard_map/all_gather | solution.py:43
  188.6 0.1 copy.58
  188.8 5.8 scatter_custom_fusion
  194.6 2.2 reshape.238
  196.8 0.0 copy-start.3
  196.8 258.6 %all_to_all.10 = bf16[64,4,4096]{2,1,0:T(4,128)(2,1)S(1)} all-to-all(bf16[64,4,4096]{2,1,0:T(4,128)(2,1)} %reshape.238), channel_id=1, replica_groups=mesh['dp'=16,'node'=4,'innode'=16] {'node','innode'}, dimensions={0} | all-to-all | bytes 4194304 | tf_op jit(solution)/shard_map/all_to_all | solution.py:63
  455.4 0.0 copy-done.3
  455.4 2.5 fusion.4
  457.9 0.0 copy-done
  457.9 5.6 convolution_convert_fusion
  463.5 4.6 copy.33
  468.1 0.0 copy-start.1
  468.1 0.0 copy-start.2
  468.1 8.1 all-to-all-start.1
  476.2 0.0 copy-done.1
  476.2 143.5 %all_gather.9 = s32[1,16,8]{2,0,1:T(1,128)S(1)} all-gather(s32[1,1,8]{2,0,1:T(1,128)S(1)} %bitcast.81), channel_id=1, replica_groups=mesh['dp'=16,'node'=4,'innode'=16] {'dp'}, dimensions={1}, use_global_device_ids=true | all-gather | bytes 544 | tf_op jit(solution)/shard_map/all_gather | solution.py:45
  619.7 0.1 copy.28
  619.8 0.1 copy.34
  619.9 1.3 dynamic-slice
  621.1 0.6 convert_reduce_fusion.1
  621.7 0.0 copy-done.2
  621.7 0.1 convert_reduce_fusion
  621.8 0.8 convolution_bitcast_fusion
  622.7 161.7 %all-reduce.1 = (f32[64]{0:T(128)S(1)}, f32[64]{0:T(128)S(1)}) all-reduce(f32[64]{0:T(128)S(1)} %convert_reduce_fusion, f32[64]{0:T(128)S(1)} %convolution_bitcast_fusion), channel_id=1, replica_groups=mesh['dp'=16,'node'=4,'innode'=16] {'dp','node','innode'}, use_global_device_ids=true, to_apply=%region_5.0 | all-reduce | flops 128 | bytes 1024 | tf_op jit(solution)/shard_map/psum | solution.py:37
  784.3 1.1 multiply_reduce_fusion.1
  785.4 0.0 all-to-all-done.1
  785.4 2.5 reshape.243
  788.0 2.2 gather_fusion
  790.2 1.6 fusion.19
  791.8 0.2 copy.57
  792.0 175.9 %all-reduce.3 = bf16[1,16,4096]{2,1,0:T(8,128)(2,1)S(1)} all-reduce(f32[1,16,4096]{2,1,0:T(8,128)S(1)} %bitcast.78), channel_id=2, replica_groups=mesh['dp'=16,'node'=4,'innode'=16] {'dp'}, use_global_device_ids=true, to_apply=%region_3.0.clone | all-reduce | flops 65536 | bytes 393216
  967.9 1.2 dynamic-slice_convert_fusion
  (5 shorter events, 0.0 us)
Async XLA Ops:
  0.6 457.3 %copy-start = (bf16[1,128,4096]{2,1,0:T(8,128)(2,1)S(1)}, bf16[1,128,4096]{2,1,0:T(8,128)(2,1)}, u32[]{:S(2)}) copy-start(bf16[1,128,4096]{2,1,0:T(8,128)(2,1)} %param.11) | copy-start | bytes 3145732
  196.8 258.6 %copy-start.3 = (bf16[1,4096,128]{2,1,0:T(8,128)(2,1)S(1)}, bf16[1,4096,128]{2,1,0:T(8,128)(2,1)}, u32[]{:S(2)}) copy-start(bf16[1,4096,128]{2,1,0:T(8,128)(2,1)} %param.9) | copy-start | bytes 3145732
  468.1 8.1 copy-start.1
  468.1 153.7 %copy-start.2 = (s32[1,1,8]{2,1,0:T(1,128)S(1)}, s32[1,1,8]{2,1,0:T(1,128)}, u32[]{:S(2)}) copy-start(s32[1,1,8]{2,1,0:T(1,128)} %param.7) | copy-start | bytes 100
  468.1 317.3 %all-to-all-start.1 = ((bf16[64,4,4096]{2,1,0:T(4,128)(2,1)}), bf16[64,4,4096]{2,1,0:T(4,128)(2,1)}, u32[]{:S(2)}, u32[]{:S(2)}) async-start(bf16[64,4,4096]{2,1,0:T(4,128)(2,1)} %copy.33), calls=%async_computation.1 | async-start | bytes 4194304 | tf_op jit(solution)/shard_map/all_to_all | solution.py:75
where the time goes:
time: 983 us; the launch traced here: 969 us
  blocking collectives  926 us (94%)
  local copies, waits for them, and re-layouts  21 us (2%)
  matrix products  10.5 us (1%)
    all_to_all x1, blocking collectives, shards(): lax.all_to_all(outgoing.reshape(experts_all, capacity, features), ('node'...  259 us
    unnamed x1, blocking collectives  176 us
    psum x1, blocking collectives, shards(): lax.psum((counts, share_sums), ('dp', 'node', 'innode'))  162 us
    all_gather x1, blocking collectives, shards(): lax.all_gather(gate_num, 'dp', axis=1, tiled=True)  143 us
    all_gather x1, blocking collectives, shards(): lax.all_gather(routes, 'dp', axis=1, tiled=True)  104 us
    all_gather x1, blocking collectives, shards(): lax.all_gather(tokens, 'dp', axis=1, tiled=True)  82 us
  transfers between devices with their start and end apart: 1, of which 0 were waited for; matrix products, arithmetic and copies ran while one was open for 0% of the time, Pallas kernels for 0%

commit v1 on v0

v1 whole, which is shorter than its diff:
```python
import functools

import jax
import jax.numpy as jnp
from jax import lax
from jax.experimental import pallas as pl
from jax.experimental.pallas import tpu as pltpu
from jax.sharding import PartitionSpec as P

GATE_DEN = 256
MESH = pl.DeviceIdType.MESH
SIDE = 4
FAR = 4


def kernel(
    dims,
    tok,
    meta,
    wg,
    wu,
    wd,
    out,
    stats,
    x3,
    mz,
    codes,
    spread,
    meta_t,
    xb,
    w1,
    w2,
    pa,
    ps,
    pr,
    h_own,
    h_oth,
    gates_t,
    ob,
    rh,
    rf,
    y3,
    rn,
    ya,
    rz,
    ssem,
    rsem,
    lsem,
):
    n_dp, feats, experts, per_token, total_tokens = dims
    ring = 2 * n_dp
    near = ring // FAR
    chunk = ring
    half = chunk // 2
    tiles = feats // 256
    part = feats // 4
    hid = wd.shape[1]
    f32, bf16 = jnp.float32, jnp.bfloat16

    dp = lax.axis_index("dp")
    node = lax.axis_index("node")
    inn = lax.axis_index("innode")
    z = lax.div(node, 2) * n_dp + dp
    core = lax.rem(node, 2)
    other = 1 - core
    py = lax.div(inn, SIDE)
    px = lax.rem(inn, SIDE)
    r = lax.rem(z, near)
    j = lax.div(z, near)

    def device(zz, cc, yy, xx):
        return (lax.rem(zz, n_dp), lax.div(zz, n_dp) * 2 + cc, yy * SIDE + xx)

    def ringz(o):
        return lax.rem(z + (o + ring), ring)

    def side(p, o):
        return lax.rem(p + (o + SIDE), SIDE)

    def slot(jj, cc):
        return lax.div(jj, 2) * chunk + r * 4 + lax.rem(jj, 2) * 2 + cc

    near_offsets = [o for o in range(-(near // 2 - 1) if near > 1 else 0, near // 2 + 1) if o != 0]
    far_steps = [(dj, dc) for dj in range(FAR) for dc in range(2) if (dj, dc) != (0, 0)]

    def far_device(dj, dc):
        jj = lax.rem(j + dj, FAR)
        cc = lax.rem(core + dc, 2)
        return jj, cc, device(r + near * jj, cc, py, px)

    barrier = pltpu.get_barrier_semaphore()
    greet = [far_device(dj, dc)[2] for dj, dc in far_steps]
    greet += [device(ringz(-o), core, py, px) for o in near_offsets]
    greet += [device(z, core, py, side(px, o)) for o in (1, 2, -1)]
    greet += [device(z, core, side(py, o), px) for o in (1, 2, -1)]
    for target in greet:
        pl.semaphore_signal(barrier, inc=1, device_id=target, device_id_type=MESH)

    local = []

    def load(src, dst):
        copy = pltpu.make_async_copy(src, dst, lsem.at[len(local)])
        copy.start()
        local.append(copy)

    def rows_of(c, h):
        return pl.ds(pl.multiple_of(c * (2 * part) + h * part, part), part)

    for h in range(2):
        load(wg.at[0, rows_of(core, h), :], w1.at[h, :, pl.ds(0, hid)])
        load(wu.at[0, rows_of(core, h), :], w1.at[h, :, pl.ds(hid, hid)])
    lanes_own = pl.ds(pl.multiple_of(core * (2 * part), 2 * part), 2 * part)
    lanes_oth = pl.ds(pl.multiple_of(other * (2 * part), 2 * part), 2 * part)
    load(wd.at[0, :, lanes_own], w2.at[pl.ds(0, hid), :])

    x3[slot(j, core)] = tok[core]
    mz[lax.div(j, 2), r * 4 + lax.rem(j, 2) * 2 + core] = meta[...]

    pl.semaphore_wait(barrier, len(greet))

    sent = {}

    def send(key, src, dst, target):
        i = len(sent)
        copy = pltpu.make_async_remote_copy(
            src_ref=src,
            dst_ref=dst,
            send_sem=ssem.at[i],
            recv_sem=rsem.at[i],
            device_id=target,
            device_id_type=MESH,
        )
        copy.start()
        sent[key] = copy

    def recv(key):
        sent[key].wait_recv()

    partner = device(z, other, py, px)

    own_slot = slot(j, core)
    own_meta = (lax.div(j, 2), r * 4 + lax.rem(j, 2) * 2 + core)
    for dj, dc in far_steps:
        jj, cc, target = far_device(dj, dc)
        send(("far", dj, dc), tok.at[cc], x3.at[own_slot], target)
    for dj, dc in far_steps:
        jj, cc, target = far_device(dj, dc)
        send(("farm", dj, dc), meta, mz.at[own_meta], target)

    for h in range(2):
        send(("wg", h), wg.at[0, rows_of(other, h), :], w1.at[h, :, pl.ds(2 * hid, hid)], partner)
        send(("wu", h), wu.at[0, rows_of(other, h), :], w1.at[h, :, pl.ds(3 * hid, hid)], partner)
    send(("wd",), wd.at[0, :, lanes_oth], w2.at[pl.ds(hid, hid), :], partner)

    for dj, dc in far_steps:
        recv(("far", dj, dc))
    for q in range(2):
        group = x3.at[pl.ds(q * chunk + r * 4, 4)]
        for o in near_offsets:
            send(("near", q, o), group, group, device(ringz(o), core, py, px))
        if q == 0:
            for dj, dc in far_steps:
                recv(("farm", dj, dc))
            group = mz.at[:, pl.ds(r * 4, 4)]
            for o in near_offsets:
                send(("nearm", o), group, group, device(ringz(o), core, py, px))

    def place(h, da, db):
        return (side(py, db), side(px, da)) if h == 0 else (side(py, da), side(px, db))

    def xy_device(h, da, db):
        yy, xx = place(h, da, db)
        return device(z, core, yy, xx)

    def block(ref, q, h, da, db, rows=None):
        yy, xx = place(h, da, db)
        return ref.at[q, h, yy, xx] if rows is None else ref.at[q, h, yy, xx, rows]

    low, high = pl.ds(0, half), pl.ds(half, half)

    def ag_own(q):
        for d in (1, -1):
            for h in range(2):
                src = block(xb, q, h, 0, 0)
                send(("p1", q, h, d), src, src, xy_device(h, d, 0))
        for h in range(2):
            ag_second(q, h, 0)

    def ag_second(q, h, a):
        src = block(xb, q, h, a, 0)
        for d in (1, -1):
            send(("p2", q, h, a, d), src, src, xy_device(h, 0, d))

    def ag_first_forward(q):
        for d in (1, -1):
            for h in range(2):
                recv(("p1", q, h, d))
                src = block(xb, q, h, -d, 0, low if d == 1 else high)
                send(("p1f", q, h, d), src, src, xy_device(h, d, 0))
                ag_second(q, h, -d)

    def ag_second_forward(q, a):
        for h in range(2):
            for d in (1, -1):
                recv(("p2", q, h, a, d))
                src = block(xb, q, h, a, -d, low if d == 1 else high)
                send(("p2f", q, h, a, d), src, src, xy_device(h, 0, d))

    def ag_opposite(q):
        for h in range(2):
            for d in (1, -1):
                recv(("p1f", q, h, d))
            ag_second(q, h, 2)

    def ag_finish(q):
        for a in (0, 1, -1, 2):
            for h in range(2):
                for d in (1, -1):
                    recv(("p2f", q, h, a, d))

    def spread_in(q):
        for o in near_offsets:
            recv(("near", q, o))
        spread[...] = x3[pl.ds(q * chunk, chunk)].astype(f32)
        per = part // 128
        for h in range(2):
            for i in range(per):
                xb[q, h, py, px, :, pl.ds(i * 128, 128)] = spread[:, h * per + i, :].astype(bf16)

    spread_in(0)
    ag_own(0)

    for o in near_offsets:
        recv(("nearm", o))
    meta_t[...] = jnp.full_like(meta_t, -1.0)
    for q in range(2):
        meta_t[pl.ds(q * chunk, chunk), :] = mz[q, :, 0, :]
    codes[py, px] = jnp.transpose(meta_t[...])[0 : 2 * per_token]
    for o in (1, -1, 2):
        src = codes.at[py, px]
        send(("mx", o), src, src, device(z, core, py, side(px, o)))

    ag_first_forward(0)
    spread_in(1)
    ag_second_forward(0, 0)
    for o in (1, -1, 2):
        recv(("mx", o))
    for o in (1, -1, 2):
        src = codes.at[py]
        send(("my", o), src, src, device(z, core, side(py, o), px))
    ag_opposite(0)
    ag_own(1)
    ag_second_forward(0, 1)
    ag_second_forward(0, -1)
    ag_first_forward(1)
    ag_second_forward(0, 2)
    ag_second_forward(1, 0)
    ag_opposite(1)

    for o in (1, -1, 2):
        recv(("my", o))
    expert = (node * (SIDE * SIDE) + inn).astype(f32)
    rows_e = lax.broadcasted_iota(jnp.int32, (experts, 128), 0).astype(f32)
    counts = jnp.zeros((experts, 128), f32)
    share_sums = jnp.zeros((experts, 128), f32)
    meta_t[...] = jnp.zeros_like(meta_t)
    for yy in range(SIDE):
        for xx in range(SIDE):
            table = codes[yy, xx]
            route, numer = table[0:per_token], table[per_token : 2 * per_token]
            valid = route >= 0
            numer = jnp.where(valid, numer, 0.0)
            total = jnp.sum(numer, axis=0, keepdims=True)
            share = numer / jnp.where(total > 0, total, 1.0)
            meta_t[pl.ds(yy * SIDE + xx, 1), :] = jnp.sum(
                jnp.where(route == expert, numer, 0.0), axis=0, keepdims=True
            ) * (1.0 / GATE_DEN)
            for k in range(per_token):
                hit = rows_e == route[k : k + 1]
                counts = counts + jnp.where(hit, 1.0, 0.0)
                share_sums = share_sums + jnp.where(hit, share[k : k + 1], 0.0)
    gates_t[...] = jnp.transpose(meta_t[...])
    load_col = jnp.sum(counts, axis=1, keepdims=True) * (experts / (per_token * total_tokens))
    mean_col = jnp.sum(share_sums, axis=1, keepdims=True) / total_tokens
    meta_t[pl.ds(0, experts), :] = jnp.broadcast_to(load_col, (experts, 128))
    stats[pl.ds(0, 1), :] = jnp.transpose(meta_t[...])[0:1]
    stats[pl.ds(1, 1), :] = jnp.broadcast_to(jnp.sum(load_col * mean_col, axis=0, keepdims=True), (1, 128))

    for copy in local:
        copy.wait()
    for h in range(2):
        recv(("wg", h))
        recv(("wu", h))
    recv(("wd",))

    rows = SIDE * chunk

    def project(q):
        def body(yy, carry):
            acc = jnp.dot(xb[q, 0, yy].reshape(rows, part), w1[0], preferred_element_type=f32)
            acc = acc + jnp.dot(xb[q, 1, yy].reshape(rows, part), w1[1], preferred_element_type=f32)
            pa[q, yy] = acc[:, 0 : 2 * hid]
            ps[q, yy] = acc[:, 2 * hid : 4 * hid]
            return carry

        lax.fori_loop(0, SIDE, body, 0)
        send(("ps", q), ps.at[q], pr.at[q], partner)

    def activate(q):
        recv(("ps", q))

        for yy in range(SIDE):
            pre = pa[q, yy] + pr[q, yy]
            gate, up = pre[:, 0:hid], pre[:, hid : 2 * hid]
            hidden = gate / (1.0 + jnp.exp(-gate)) * up
            for xx in range(SIDE):
                i = yy * SIDE + xx
                column = gates_t[pl.ds(q * chunk, chunk), pl.ds(i, 1)]
                piece = hidden[xx * chunk : (xx + 1) * chunk] * column
                h_own[q, yy, pl.ds(xx * chunk, chunk), :] = piece.astype(bf16)
        send(("h", q), h_own.at[q], h_oth.at[q], partner)

    def expand(q):
        recv(("h", q))

        def body(i, carry):
            yy = lax.rem(py + 2 + i, SIDE)
            hidden = jnp.concatenate([h_own[q, yy], h_oth[q, yy]], axis=1)
            for h in range(2):
                val = jnp.dot(hidden, w2[:, h * part : (h + 1) * part], preferred_element_type=f32)
                ob[q, h, yy] = val.astype(bf16).reshape(SIDE, chunk, part)
            return carry

        lax.fori_loop(0, SIDE, body, 0)

    index_of = {0: 0, 1: 1, -1: 2, 2: 3}

    def add_half(q, h, da, db, rows_, src):
        yy, xx = place(h, da, db)
        ob[q, h, yy, xx, rows_] = ob[q, h, yy, xx, rows_] + src

    def rs_far(q, a):
        for h in range(2):
            for d in (1, -1):
                src = block(ob, q, h, a, 2, low if d == 1 else high)
                send(("r1", q, h, a, d), src, rh.at[q, h, index_of[a], (1 - d) // 2], xy_device(h, 0, d))

    def rs_side(q, a):
        for h in range(2):
            for d in (1, -1):
                recv(("r1", q, h, a, d))
                add_half(q, h, a, d, low if d == 1 else high, rh[q, h, index_of[a], (1 - d) // 2])
                send(
                    ("r2", q, h, a, d),
                    block(ob, q, h, a, d),
                    rf.at[q, h, index_of[a], (1 - d) // 2],
                    xy_device(h, 0, d),
                )

    def rs_take(q, h, a):
        for d in (1, -1):
            recv(("r2", q, h, a, d))
        i = index_of[a]
        yy, xx = place(h, a, 0)
        total = ob[q, h, yy, xx].astype(f32) + rf[q, h, i, 0].astype(f32) + rf[q, h, i, 1].astype(f32)
        ob[q, h, yy, xx] = total.astype(bf16)

    def rs_second_far(q):
        for h in range(2):
            rs_take(q, h, 2)
            for d in (1, -1):
                src = block(ob, q, h, 2, 0, low if d == 1 else high)
                send(("r3", q, h, d), src, rh.at[q, h, 4, (1 - d) // 2], xy_device(h, d, 0))

    def rs_second_side(q):
        for h in range(2):
            for d in (1, -1):
                rs_take(q, h, d)
                recv(("r3", q, h, d))
                add_half(q, h, d, 0, low if d == 1 else high, rh[q, h, 4, (1 - d) // 2])
                send(("r4", q, h, d), block(ob, q, h, d, 0), rf.at[q, h, 4, (1 - d) // 2], xy_device(h, d, 0))

    def rs_last(q):
        per = part // 128
        for h in range(2):
            rs_take(q, h, 0)
            for d in (1, -1):
                recv(("r4", q, h, d))
            total = ob[q, h, py, px].astype(f32) + rf[q, h, 4, 0].astype(f32) + rf[q, h, 4, 1].astype(f32)
            for i in range(per):
                spread[:, h * per + i, :] = total[:, i * 128 : (i + 1) * 128]
        y3[q] = spread[...].astype(bf16)

    def z_near(q):
        for o in near_offsets:
            src = y3.at[q, pl.ds(lax.rem(r + (o + near), near) * 4, 4)]
            send(("zn", q, o), src, rn.at[q, near_offsets.index(o)], device(ringz(o), core, py, px))

    def z_take(q):
        for o in near_offsets:
            recv(("zn", q, o))
        total = y3[q, pl.ds(r * 4, 4)].astype(f32)
        for i in range(len(near_offsets)):
            total = total + rn[q, i].astype(f32)
        ya[pl.ds(q * 4, 4)] = total.astype(bf16)

    ag_finish(0)
    project(0)
    ag_second_forward(1, 1)
    ag_second_forward(1, -1)
    activate(0)
    ag_second_forward(1, 2)
    expand(0)
    for a in (2, 1, -1, 0):
        rs_far(0, a)
    ag_finish(1)
    project(1)
    rs_side(0, 2)
    activate(1)
    rs_side(0, 1)
    rs_side(0, -1)
    rs_side(0, 0)
    expand(1)
    for a in (2, 1, -1, 0):
        rs_far(1, a)
    rs_second_far(0)
    rs_second_side(0)
    for a in (2, 1, -1, 0):
        rs_side(1, a)
    rs_last(0)
    z_near(0)
    rs_second_far(1)
    rs_second_side(1)
    z_take(0)
    rs_last(1)
    z_near(1)
    z_take(1)

    for dj, dc in far_steps:
        jj, cc, target = far_device(dj, dc)
        send(("zf", dj, dc), ya.at[jj * 2 + cc], rz.at[dj * 2 + dc], target)
    for dj, dc in far_steps:
        recv(("zf", dj, dc))
    same = ya[j * 2 + core].astype(f32)
    cross = jnp.zeros_like(same)
    for dj in range(FAR):
        if dj:
            same = same + rz[dj * 2].astype(f32)
        cross = cross + rz[dj * 2 + 1].astype(f32)
    out[core] = same.astype(bf16)
    out[other] = cross.astype(bf16)

    for copy in sent.values():
        copy.wait_send()


def solution(mesh):
    n_dp = mesh.shape["dp"]

    def shards(tokens, routes, gate_num, w_gate, w_up, w_down):
        feats = tokens.shape[2]
        per_token = routes.shape[2]
        hid = w_down.shape[1]
        experts = mesh.shape["node"] * mesh.shape["innode"]
        ring = 2 * n_dp
        chunk, near = ring, ring // FAR
        tiles, part = feats // 256, feats // 4
        dims = (n_dp, feats, experts, per_token, n_dp * experts)
        tok = tokens.reshape(2, tiles, 128)
        meta = jnp.concatenate([routes[0], gate_num[0]], axis=1).astype(jnp.float32)
        meta = jnp.pad(meta, ((0, 0), (0, 128 - 2 * per_token)))
        bf16, f32 = jnp.bfloat16, jnp.float32
        copies = 400
        vm = pltpu.VMEM
        out, stats = pl.pallas_call(
            functools.partial(kernel, dims),
            out_shape=(
                jax.ShapeDtypeStruct((2, tiles, 128), bf16),
                jax.ShapeDtypeStruct((8, 128), f32),
            ),
            in_specs=[pl.BlockSpec(memory_space=pltpu.VMEM)] * 2 + [pl.BlockSpec(memory_space=pl.ANY)] * 3,
            out_specs=[pl.BlockSpec(memory_space=pltpu.VMEM)] * 2,
            scratch_shapes=[
                vm((2 * chunk, tiles, 128), bf16),
                vm((2, chunk, 1, 128), f32),
                vm((SIDE, SIDE, 2 * per_token, 128), f32),
                vm((chunk, tiles, 128), f32),
                vm((128, 128), f32),
                vm((2, 2, SIDE, SIDE, chunk, part), bf16),
                vm((2, part, 4 * hid), bf16),
                vm((2 * hid, 2 * part), bf16),
                vm((2, SIDE, SIDE * chunk, 2 * hid), f32),
                vm((2, SIDE, SIDE * chunk, 2 * hid), f32),
                vm((2, SIDE, SIDE * chunk, 2 * hid), f32),
                vm((2, SIDE, SIDE * chunk, hid), bf16),
                vm((2, SIDE, SIDE * chunk, hid), bf16),
                vm((128, 128), f32),
                vm((2, 2, SIDE, SIDE, chunk, part), bf16),
                vm((2, 2, 5, 2, chunk // 2, part), bf16),
                vm((2, 2, 5, 2, chunk, part), bf16),
                vm((2, chunk, tiles, 128), bf16),
                vm((2, max(1, near - 1), 4, tiles, 128), bf16),
                vm((8, tiles, 128), bf16),
                vm((8, tiles, 128), bf16),
                pltpu.SemaphoreType.DMA((copies,)),
                pltpu.SemaphoreType.DMA((copies,)),
                pltpu.SemaphoreType.DMA((8,)),
            ],
            compiler_params=pltpu.CompilerParams(
                collective_id=0, has_side_effects=True, vmem_limit_bytes=50 * 1024 * 1024
            ),
            name="expert_layer",
        )(tok, meta, w_gate, w_up, w_down)
        return out.reshape(1, 1, feats), stats[0, :experts], stats[1, 0]

    column = P(("node", "innode"), "dp", None)
    in_specs = (column, column, column, P(("node", "innode"), None, "dp"), P(("node", "innode"), None, "dp"), column)
    return jax.shard_map(shards, mesh=mesh, in_specs=in_specs, out_specs=(column, P(), P()), check_vma=False)
```

time: 983 us -> 138 us (0.14); the launches traced: 969 us -> 138 us
  blocking collectives: 926 us -> 0 us
  Pallas kernels: 0 us -> 130 us
  local copies, waits for them, and re-layouts: 21 us -> 5.97 us
  matrix products: 10.5 us -> 0 us
    all_gather x3 -> x0, blocking collectives: 330 us -> none  [the longest x1 143 us: shards(): lax.all_gather(gate_num, 'dp', axis=1, tiled=True)]
    all_to_all x1 -> x0, blocking collectives: 259 us -> none  [shards(): lax.all_to_all(outgoing.reshape(experts_all, capacity, features), ('node'...]
    unnamed x1 -> x0, blocking collectives: 176 us -> none
    psum x1 -> x0, blocking collectives: 162 us -> none  [shards(): lax.psum((counts, share_sums), ('dp', 'node', 'innode'))]
    pallas_call x0 -> x1, Pallas kernels: none -> 130 us  [shards(): pl.pallas_call(functools.partial(kernel, dims), out_shape=(jax.ShapeDtype...]
    dot_general x4 -> x0, matrix products: 10.5 us -> none  [the longest x1 5.57 us: apply_experts(): jnp.einsum('sekh,ehd->sekd', hidden, w_down, preferred_element_type=jnp.f...]
  transfers between devices with their start and end apart: 1 -> 0, of which waited for: 0 -> 0; matrix products, arithmetic and copies ran while one was open for 0% -> 0% of each run, Pallas kernels for 0% -> 0%
where the time goes in v1:
time: 138 us
  Pallas kernels  130 us (94%)
  local copies, waits for them, and re-layouts  5.97 us (4%)
    pallas_call x1, Pallas kernels, shards(): pl.pallas_call(functools.partial(kernel, dims), out_shape=(jax.ShapeDtype...  130 us
    unnamed x10, local copies, waits for them, and re-layouts  4.32 us

profile of v1, /device:TPU:1, one launch (start us, length us, event | category | flops | bytes accessed | tf_op | source)
XLA Modules:
  0.0 137.5 jit_solution(7992913338842974619)
XLA Ops:
  0.6 0.0 copy-start.3
  0.6 0.0 copy-start.4
  0.7 0.6 copy-done.3
  1.3 0.0 copy-done.4
  1.3 0.1 add_convert_fusion
  1.4 0.8 reduce
  2.2 0.0 copy-start
  2.2 1.2 copy-done
  3.4 0.0 copy-start.1
  3.4 1.2 copy-done.1
  4.6 0.0 copy-start.2
  4.6 1.2 copy-done.2
  5.8 130.1 %expert_layer.1 = (bf16[2,16,128]{2,1,0:T(8,128)(2,1)S(1)}, f32[8,128]{1,0:T(8,128)S(1)}) custom-call(bf16[2,16,128]{2,1,0:T(8,128)(2,1)S(1)} %bitcast.6, f32[1,128]{1,0:T(1,128)S(1)} %pad.4.meta, bf16[1,4096,128]{2,1,0:T(8,128)(2,1)S(1)} %copy-done, bf16[1,4096,128]{2,1,0:T(8,128)(2,1)S(1)} %copy-done.1, bf16[1,128,4096]{2,1,0:T(8,128)(2,1)S(1)} %copy-done.2), custom_call_target="tpu_custom_call" | custom-call | tf_op jit(solution)/shard_map/expert_layer/pallas_call | solution.py:475
  135.9 0.5 slice.7
  136.4 0.5 slice_bitcast_fusion
  136.9 0.6 reshape.49
  (1 shorter events, 0.0 us)
Async XLA Ops:
  0.6 0.7 copy-start.3
  0.6 0.7 copy-start.4
  2.2 1.2 copy-start
  3.4 1.2 copy-start.1
  4.6 1.2 copy-start.2

commit v2 on v0

v2 whole, which is shorter than its diff:
```python
import functools

import jax
import jax.numpy as jnp
from jax import lax
from jax.experimental import pallas as pl
from jax.experimental.pallas import tpu as pltpu
from jax.sharding import PartitionSpec as P

GATE_DEN = 256
MESH = pl.DeviceIdType.MESH
SIDE = 4
N_SEND, N_RECV = 33, 102
FAR = 4


def kernel(
    dims,
    tokens,
    routes,
    gate_num,
    wg,
    wu,
    wd,
    out,
    load_out,
    loss_out,
    tok_in,
    routes_in,
    gates_in,
    tok,
    rows_f,
    pair,
    pair_m,
    x3,
    mz,
    codes,
    spread,
    meta_t,
    xb,
    w1,
    w2,
    pa,
    ps,
    pr,
    h_own,
    h_oth,
    gates_t,
    ob,
    rh,
    rf,
    y3,
    rn,
    ya,
    rz,
    fin,
    ssem,
    rsem,
    lsem,
):
    n_dp, feats, experts, per_token, total_tokens = dims
    ring = 2 * n_dp
    near = ring // FAR
    chunk = ring
    half = chunk // 2
    tiles = feats // 256
    part = feats // 4
    hid = wd.shape[1]
    f32, bf16 = jnp.float32, jnp.bfloat16

    dp = lax.axis_index("dp")
    node = lax.axis_index("node")
    inn = lax.axis_index("innode")
    z = lax.div(node, 2) * n_dp + dp
    core = lax.rem(node, 2)
    other = 1 - core
    py = lax.div(inn, SIDE)
    px = lax.rem(inn, SIDE)

    def device(zz, cc, yy, xx):
        return (lax.rem(zz, n_dp), lax.div(zz, n_dp) * 2 + cc, yy * SIDE + xx)

    def ringz(o):
        return lax.rem(z + (o + ring), ring)

    def side(p, o):
        return lax.rem(p + (o + SIDE), SIDE)

    far = [3 * near // 2, -3 * near // 2, near // 2, -near // 2]
    steps = sorted(range(-near // 2, near // 2), key=abs)
    members = 2 * FAR
    per_chunk = near // 2

    def along(o):
        return device(ringz(o), core, py, px)

    partner = device(z, other, py, px)

    barrier = pltpu.get_barrier_semaphore()
    greet = [along(f) for f in far]
    greet += [along(o) for o in range(near // 2, 0, -1)] + [along(-o) for o in range(near // 2, 0, -1)]
    greet = greet if near > 2 else greet[:2] + [along(1), along(-1)]
    greet += [device(z, core, py, side(px, o)) for o in (1, -1)]
    greet += [device(z, core, side(py, o), px) for o in (1, -1)]
    greet += [partner]
    for target in greet:
        pl.semaphore_signal(barrier, inc=1, device_id=target, device_id_type=MESH)

    def load(src, dst, i):
        copy = pltpu.make_async_copy(src, dst, lsem.at[i])
        copy.start()
        return copy

    def rows_of(c, h):
        return pl.ds(pl.multiple_of(c * (2 * part) + h * part, part), part)

    def lanes_of(c):
        return pl.ds(pl.multiple_of(c * (2 * part), 2 * part), 2 * part)

    small = [load(tokens, tok_in, 0), load(routes, routes_in, 1), load(gate_num, gates_in, 2)]
    for h in range(2):
        load(wg.at[0, rows_of(core, h), :], w1.at[h, :, pl.ds(0, hid)], 3)
        load(wu.at[0, rows_of(core, h), :], w1.at[h, :, pl.ds(hid, hid)], 3)
    load(wd.at[0, :, lanes_of(core)], w2.at[pl.ds(0, hid), :], 4)

    for copy in small:
        copy.wait()
    for i in range(2 * tiles):
        rows_f[pl.ds(i, 1), :] = tok_in[0, :, pl.ds(i * 128, 128)].astype(f32)
    for h in range(2):
        tok[h] = rows_f[pl.ds(h * tiles, tiles), :].astype(bf16)
    pair[core] = tok[core]
    pair_m[core] = jnp.concatenate(
        [
            routes_in[0].astype(f32),
            gates_in[0].astype(f32),
            jnp.zeros((1, 128 - 2 * per_token), f32),
        ],
        axis=1,
    )

    pl.semaphore_wait(barrier, len(greet))

    sends, recvs = {}, {}

    def send(name, src, dst, target, arrival=None, departure=None):
        arrival = name if arrival is None else arrival
        departure = name if departure is None else departure
        pltpu.make_async_remote_copy(
            src_ref=src,
            dst_ref=dst,
            send_sem=ssem.at[sends.setdefault(departure, len(sends))],
            recv_sem=rsem.at[recvs.setdefault(arrival, len(recvs))],
            device_id=target,
            device_id_type=MESH,
        ).start()

    def end_of(like, s_index, r_index):
        return pltpu.make_async_remote_copy(
            src_ref=like,
            dst_ref=like,
            send_sem=ssem.at[s_index],
            recv_sem=rsem.at[r_index],
            device_id=partner,
            device_id_type=MESH,
        )

    def arrived(name, like):
        end_of(like, 0, recvs[name]).wait_recv()

    def departed(name, like):
        end_of(like, sends.pop(name), 0).wait_send()

    send("pair", tok.at[other], pair.at[core], partner)
    send("pairm", pair_m.at[core], pair_m.at[core], partner)
    arrived("pair", tok.at[0])
    for i, f in enumerate(far):
        send("far", pair, x3.at[pl.ds(2 * i, 2)], along(f))
    arrived("pairm", pair_m.at[0])
    for i, f in enumerate(far):
        send("farm", pair_m, mz.at[pl.ds(2 * i, 2)], along(f))

    for h in range(2):
        send("w1", wg.at[0, rows_of(other, h), :], w1.at[h, :, pl.ds(2 * hid, hid)], partner)
        send("w1", wu.at[0, rows_of(other, h), :], w1.at[h, :, pl.ds(3 * hid, hid)], partner)
    send("w2", wd.at[0, :, lanes_of(other)], w2.at[pl.ds(hid, hid), :], partner)

    near_rest = pl.ds(members, (near - 1) * members)
    arrived("far", x3.at[pl.ds(0, members)])
    for g in range(1, near):
        send("near", x3.at[pl.ds(0, members)], x3.at[pl.ds(g * members, members)], along(steps[g]), ("near", g // per_chunk))
    arrived("farm", mz.at[pl.ds(0, members)])
    for g in range(1, near):
        send("nearm", mz.at[pl.ds(0, members)], mz.at[pl.ds(g * members, members)], along(steps[g]))

    def place(h, da, db):
        return (side(py, db), side(px, da)) if h == 0 else (side(py, da), side(px, db))

    def xy_device(h, da, db):
        yy, xx = place(h, da, db)
        return device(z, core, yy, xx)

    def block(ref, q, h, da, db, rows=None):
        yy, xx = place(h, da, db)
        return ref.at[q, h, yy, xx] if rows is None else ref.at[q, h, yy, xx, rows]

    low, high = pl.ds(0, half), pl.ds(half, half)

    def ag_own(q):
        for h in range(2):
            for d in (1, -1):
                src = block(xb, q, h, 0, 0)
                send(("p1", q, h), src, src, xy_device(h, d, 0), None, ("full", q, h))
        for h in range(2):
            ag_second(q, h, 0)

    def ag_second(q, h, a):
        src = block(xb, q, h, a, 0)
        for d in (1, -1):
            send(("p2", q, h, a), src, src, xy_device(h, 0, d), None, ("full", q, h))

    def ag_first_forward(q):
        for h in range(2):
            arrived(("p1", q, h), rf.at[q, h, 0])
            for d in (1, -1):
                src = block(xb, q, h, -d, 0, low if d == 1 else high)
                send(("p1f", q, h), src, src, xy_device(h, d, 0), None, ("half", q, h))
            for d in (1, -1):
                ag_second(q, h, -d)

    def ag_second_forward(q, a):
        for h in range(2):
            arrived(("p2", q, h, a), rf.at[q, h, 0])
            for d in (1, -1):
                src = block(xb, q, h, a, -d, low if d == 1 else high)
                send(("p2f", q, h), src, src, xy_device(h, 0, d), None, ("half", q, h))

    def ag_opposite(q):
        for h in range(2):
            arrived(("p1f", q, h), block(xb, q, h, 2, 0))
            ag_second(q, h, 2)

    def ag_finish(q):
        for h in range(2):
            arrived(("p2f", q, h), rh.at[q, h, pl.ds(0, SIDE)])

    def spread_in(q):
        first = members if q == 0 else 0
        arrived(("near", q), x3.at[pl.ds(q * chunk + first, chunk - first)])
        spread[...] = x3[pl.ds(q * chunk, chunk)].astype(f32)
        per = part // 128
        for h in range(2):
            for i in range(per):
                xb[q, h, py, px, :, pl.ds(i * 128, 128)] = spread[:, h * per + i, :].astype(bf16)

    turn = (2, 1, -1, 0)

    def project(q):
        for t in turn:
            yy = side(py, t)
            acc = jnp.dot(xb[q, 0, yy].reshape(SIDE * chunk, part), w1[0], preferred_element_type=f32)
            acc = acc + jnp.dot(xb[q, 1, yy].reshape(SIDE * chunk, part), w1[1], preferred_element_type=f32)
            pa[q, yy] = acc[:, 0 : 2 * hid]
            ps[q, yy] = acc[:, 2 * hid : 4 * hid]
            send(("ps", q, t), ps.at[q, yy], pr.at[q, yy], partner, None, ("ps", q))

    def activate(q):
        for t in turn:
            yy = side(py, t)
            arrived(("ps", q, t), ps.at[q, 0])
            pre = pa[q, yy] + pr[q, yy]
            gate, up = pre[:, 0:hid], pre[:, hid : 2 * hid]
            hidden = gate / (1.0 + jnp.exp(-gate)) * up
            for xx in range(SIDE):
                column = gates_t[q, yy, pl.ds(xx * chunk, chunk), :]
                piece = hidden[xx * chunk : (xx + 1) * chunk] * column
                h_own[q, yy, pl.ds(xx * chunk, chunk), :] = piece.astype(bf16)
            send(("h", q, t), h_own.at[q, yy], h_oth.at[q, yy], partner, None, ("h", q))

    index_of = {0: 0, 1: 1, -1: 2, 2: 3}

    def expand(q):
        for t in turn:
            yy = side(py, t)
            arrived(("h", q, t), h_own.at[q, 0])
            hidden = jnp.concatenate([h_own[q, yy], h_oth[q, yy]], axis=1)
            for h in range(2):
                val = jnp.dot(hidden, w2[:, h * part : (h + 1) * part], preferred_element_type=f32)
                ob[q, h, yy] = val.astype(bf16).reshape(SIDE, chunk, part)
            if t == 2:
                for a in turn:
                    rs_far(q, 0, a)
            rs_far(q, 1, t)

    def rs_far(q, h, a):
        for d in (1, -1):
            src = block(ob, q, h, a, 2, low if d == 1 else high)
            dst = rh.at[q, h, index_of[a], (1 - d) // 2]
            send(("r1", q, h, a), src, dst, xy_device(h, 0, d), None, ("rhalf", q, h))

    def add_half(q, h, da, db, rows, src):
        yy, xx = place(h, da, db)
        ob[q, h, yy, xx, rows] = ob[q, h, yy, xx, rows] + src

    def rs_side(q, a):
        for h in range(2):
            i = index_of[a]
            arrived(("r1", q, h, a), rh.at[q, h, i])
            for d in (1, -1):
                add_half(q, h, a, d, low if d == 1 else high, rh[q, h, i, (1 - d) // 2])
                dst = rf.at[q, h, i, (1 - d) // 2]
                send(("r2", q, h, a), block(ob, q, h, a, d), dst, xy_device(h, 0, d), None, ("rfull", q, h))

    def rs_take(q, h, a):
        i = index_of[a]
        arrived(("r2", q, h, a), rf.at[q, h, i])
        yy, xx = place(h, a, 0)
        return ob[q, h, yy, xx].astype(f32) + rf[q, h, i, 0].astype(f32) + rf[q, h, i, 1].astype(f32)

    def rs_second_far(q):
        for h in range(2):
            yy, xx = place(h, 2, 0)
            ob[q, h, yy, xx] = rs_take(q, h, 2).astype(bf16)
            for d in (1, -1):
                src = block(ob, q, h, 2, 0, low if d == 1 else high)
                dst = rh.at[q, h, 4, (1 - d) // 2]
                send(("r3", q, h), src, dst, xy_device(h, d, 0), None, ("rhalf", q, h))

    def rs_second_side(q):
        for h in range(2):
            for d in (1, -1):
                yy, xx = place(h, d, 0)
                ob[q, h, yy, xx] = rs_take(q, h, d).astype(bf16)
        for h in range(2):
            arrived(("r3", q, h), rh.at[q, h, 4])
            for d in (1, -1):
                add_half(q, h, d, 0, low if d == 1 else high, rh[q, h, 4, (1 - d) // 2])
                dst = rf.at[q, h, 4, (1 - d) // 2]
                send(("r4", q, h), block(ob, q, h, d, 0), dst, xy_device(h, d, 0), None, ("rfull", q, h))

    def rs_last(q):
        per = part // 128
        for h in range(2):
            total = rs_take(q, h, 0)
            arrived(("r4", q, h), rf.at[q, h, 4])
            total = total + rf[q, h, 4, 0].astype(f32) + rf[q, h, 4, 1].astype(f32)
            for i in range(per):
                spread[:, h * per + i, :] = total[:, i * 128 : (i + 1) * 128]
        y3[q] = spread[...].astype(bf16)
        for g in range(q * per_chunk, (q + 1) * per_chunk):
            if g:
                src = y3.at[q, pl.ds((g - q * per_chunk) * members, members)]
                send("zn", src, rn.at[g - 1], along(-steps[g]))

    def statistics():
        rows_e = lax.broadcasted_iota(jnp.int32, (experts, 128), 0).astype(f32)

        def body(i, carry):
            counts, share_sums = carry
            table = codes[lax.div(i, SIDE), lax.rem(i, SIDE)]
            route, numer = table[0:per_token], table[per_token : 2 * per_token]
            numer = jnp.where(route >= 0, numer, 0.0)
            total = jnp.sum(numer, axis=0, keepdims=True)
            share = numer / jnp.where(total > 0, total, 1.0)
            for k in range(per_token):
                hit = rows_e == route[k : k + 1]
                counts = counts + jnp.where(hit, 1.0, 0.0)
                share_sums = share_sums + jnp.where(hit, share[k : k + 1], 0.0)
            return counts, share_sums

        zero = jnp.zeros((experts, 128), f32)
        counts, share_sums = lax.fori_loop(0, SIDE * SIDE, body, (zero, zero))
        load_col = jnp.sum(counts, axis=1, keepdims=True) * (experts / (per_token * total_tokens))
        mean_col = jnp.sum(share_sums, axis=1, keepdims=True) / total_tokens
        meta_t[pl.ds(0, experts), :] = jnp.broadcast_to(load_col, (experts, 128))
        load_out[...] = jnp.transpose(meta_t[...])[0:1, 0:experts]
        loss_out[...] = jnp.sum(load_col * mean_col, axis=0, keepdims=True)

    def codes_own():
        arrived("nearm", mz.at[near_rest])
        meta_t[...] = jnp.full_like(meta_t, -1.0)
        meta_t[pl.ds(0, 2 * chunk), :] = mz[:, 0, :]
        codes[py, px] = jnp.transpose(meta_t[...])[0 : 2 * per_token]
        for o in (1, -1):
            src = codes.at[py, px]
            send(("mx", o), src, src, device(z, core, py, side(px, o)), None, "mx")

    def codes_x():
        arrived(("mx", 1), codes.at[0, 0])
        src = codes.at[py, side(px, -1)]
        send(("mx", 2), src, src, device(z, core, py, side(px, 1)), None, "mx")

    def codes_row():
        arrived(("mx", -1), codes.at[0, 0])
        arrived(("mx", 2), codes.at[0, 0])
        for o in (1, -1):
            src = codes.at[py]
            send(("my", o), src, src, device(z, core, side(py, o), px), None, "my")

    def codes_y():
        arrived(("my", 1), codes.at[0])
        src = codes.at[side(py, -1)]
        send(("my", 2), src, src, device(z, core, side(py, 1), px), None, "my")

    def gates():
        arrived(("my", -1), codes.at[0])
        arrived(("my", 2), codes.at[0])
        expert = (node * (SIDE * SIDE) + inn).astype(f32)
        meta_t[...] = jnp.zeros_like(meta_t)
        for yy in range(SIDE):
            for xx in range(SIDE):
                route, numer = codes[yy, xx, 0:per_token], codes[yy, xx, per_token : 2 * per_token]
                meta_t[pl.ds(yy * SIDE + xx, 1), :] = jnp.sum(
                    jnp.where(route == expert, numer, 0.0), axis=0, keepdims=True
                ) * (1.0 / GATE_DEN)
        columns = jnp.transpose(meta_t[...])
        for q in range(2):
            for yy in range(SIDE):
                for xx in range(SIDE):
                    i = yy * SIDE + xx
                    column = columns[q * chunk : (q + 1) * chunk, i : i + 1]
                    gates_t[q, yy, pl.ds(xx * chunk, chunk), :] = jnp.broadcast_to(column, (chunk, hid))

    spread_in(0)
    ag_own(0)
    spread_in(1)
    ag_own(1)
    codes_own()
    ag_first_forward(0)
    ag_second_forward(0, 0)
    ag_opposite(0)
    codes_x()
    ag_first_forward(1)
    ag_second_forward(0, 1)
    ag_second_forward(0, -1)
    codes_row()
    ag_second_forward(1, 0)
    ag_opposite(1)
    ag_second_forward(0, 2)
    codes_y()
    pltpu.make_async_copy(w1.at[:, :, pl.ds(0, 2 * hid)], w1.at[:, :, pl.ds(0, 2 * hid)], lsem.at[3]).wait()
    pltpu.make_async_copy(w2.at[pl.ds(0, hid), :], w2.at[pl.ds(0, hid), :], lsem.at[4]).wait()
    arrived("w1", w1.at[:, :, pl.ds(2 * hid, 2 * hid)])
    arrived("w2", w2.at[pl.ds(hid, hid), :])
    gates()

    ag_finish(0)
    project(0)
    ag_second_forward(1, 1)
    ag_second_forward(1, -1)
    activate(0)
    ag_second_forward(1, 2)
    expand(0)
    ag_finish(1)
    project(1)
    rs_side(0, 2)
    activate(1)
    rs_side(0, 1)
    rs_side(0, -1)
    rs_side(0, 0)
    expand(1)
    rs_second_far(0)
    rs_second_side(0)
    rs_side(1, 2)
    rs_side(1, 1)
    rs_side(1, -1)
    rs_side(1, 0)
    rs_last(0)
    rs_second_far(1)
    rs_second_side(1)
    rs_last(1)

    arrived("zn", rn)
    total = y3[0, pl.ds(0, members)].astype(f32)
    for g in range(near - 1):
        total = total + rn[g].astype(f32)
    ya[...] = total.astype(bf16)
    for i, f in enumerate(far):
        send("zf", ya.at[pl.ds(2 * i, 2)], rz.at[i], along(-f))
    statistics()
    for q in range(2):
        for h in range(2):
            departed(("full", q, h), rf.at[q, h])
            departed(("half", q, h), rh.at[q, h])
            departed(("rfull", q, h), rf.at[q, h])
            departed(("rhalf", q, h), rh.at[q, h])
        departed(("ps", q), ps.at[q])
        departed(("h", q), h_own.at[q])
    departed("pair", tok.at[0])
    departed("pairm", pair_m.at[0])
    departed("far", x3.at[pl.ds(0, members)])
    departed("farm", mz.at[pl.ds(0, members)])
    departed("near", x3.at[near_rest])
    departed("nearm", mz.at[near_rest])
    departed("w1", w1.at[:, :, pl.ds(2 * hid, 2 * hid)])
    departed("w2", w2.at[pl.ds(hid, hid), :])
    departed("mx", codes.at[0, pl.ds(0, 3)])
    departed("my", codes.at[pl.ds(0, 3)])
    departed("zn", rn)
    departed("zf", rz)
    arrived("zf", rz)

    def gathered(c):
        return rz[0, c].astype(f32) + rz[1, c].astype(f32) + rz[2, c].astype(f32) + rz[3, c].astype(f32)

    fin[other] = gathered(other).astype(bf16)
    send("fin", fin.at[other], fin.at[other], partner)
    rows_f[pl.ds(pl.multiple_of(core * tiles, tiles), tiles), :] = gathered(core)
    arrived("fin", fin.at[0])
    rows_f[pl.ds(pl.multiple_of(other * tiles, tiles), tiles), :] = fin[core].astype(f32)
    for i in range(2 * tiles):
        out[0, :, pl.ds(i * 128, 128)] = rows_f[pl.ds(i, 1), :].astype(bf16)
    departed("fin", fin.at[0])


def solution(mesh):
    n_dp = mesh.shape["dp"]

    def shards(tokens, routes, gate_num, w_gate, w_up, w_down):
        feats = tokens.shape[2]
        per_token = routes.shape[2]
        hid = w_down.shape[1]
        experts = mesh.shape["node"] * mesh.shape["innode"]
        ring = 2 * n_dp
        chunk, near = ring, ring // FAR
        tiles, part = feats // 256, feats // 4
        dims = (n_dp, feats, experts, per_token, n_dp * experts)
        bf16, f32 = jnp.bfloat16, jnp.float32
        vm = pltpu.VMEM
        out, load, loss = pl.pallas_call(
            functools.partial(kernel, dims),
            out_shape=(
                jax.ShapeDtypeStruct((1, 1, feats), bf16),
                jax.ShapeDtypeStruct((1, experts), f32),
                jax.ShapeDtypeStruct((1, 1), f32),
            ),
            in_specs=[pl.BlockSpec(memory_space=pltpu.HBM)] * 6,
            out_specs=[pl.BlockSpec(memory_space=pltpu.VMEM)] * 3,
            scratch_shapes=[
                vm((1, 1, feats), bf16),
                vm((1, 1, per_token), jnp.int32),
                vm((1, 1, per_token), jnp.int32),
                vm((2, tiles, 128), bf16),
                vm((2 * tiles, 128), f32),
                vm((2, tiles, 128), bf16),
                vm((2, 1, 128), f32),
                vm((2 * chunk, tiles, 128), bf16),
                vm((2 * chunk, 1, 128), f32),
                vm((SIDE, SIDE, 2 * per_token, 128), f32),
                vm((chunk, tiles, 128), f32),
                vm((128, 128), f32),
                vm((2, 2, SIDE, SIDE, chunk, part), bf16),
                vm((2, part, 4 * hid), bf16),
                vm((2 * hid, 2 * part), bf16),
                vm((2, SIDE, SIDE * chunk, 2 * hid), f32),
                vm((2, SIDE, SIDE * chunk, 2 * hid), f32),
                vm((2, SIDE, SIDE * chunk, 2 * hid), f32),
                vm((2, SIDE, SIDE * chunk, hid), bf16),
                vm((2, SIDE, SIDE * chunk, hid), bf16),
                vm((2, SIDE, SIDE * chunk, hid), f32),
                vm((2, 2, SIDE, SIDE, chunk, part), bf16),
                vm((2, 2, 5, 2, chunk // 2, part), bf16),
                vm((2, 2, 5, 2, chunk, part), bf16),
                vm((2, chunk, tiles, 128), bf16),
                vm((near - 1, 2 * FAR, tiles, 128), bf16),
                vm((2 * FAR, tiles, 128), bf16),
                vm((FAR, 2, tiles, 128), bf16),
                vm((2, tiles, 128), bf16),
                pltpu.SemaphoreType.DMA((N_SEND,)),
                pltpu.SemaphoreType.DMA((N_RECV,)),
                pltpu.SemaphoreType.DMA((5,)),
            ],
            compiler_params=pltpu.CompilerParams(
                collective_id=0, has_side_effects=True, vmem_limit_bytes=63 * 1024 * 1024
            ),
            name="expert_layer",
        )(tokens, routes, gate_num, w_gate, w_up, w_down)
        return out, load.reshape(experts), loss.reshape(())

    column = P(("node", "innode"), "dp", None)
    in_specs = (column, column, column, P(("node", "innode"), None, "dp"), P(("node", "innode"), None, "dp"), column)
    return jax.shard_map(shards, mesh=mesh, in_specs=in_specs, out_specs=(column, P(), P()), check_vma=False)
```

time: 983 us -> 127 us (0.13); the launches traced: 969 us -> 127 us
  blocking collectives: 926 us -> 0 us
  Pallas kernels: 0 us -> 123 us
  local copies, waits for them, and re-layouts: 21 us -> 1.86 us
  matrix products: 10.5 us -> 0 us
    all_gather x3 -> x0, blocking collectives: 330 us -> none  [the longest x1 143 us: shards(): lax.all_gather(gate_num, 'dp', axis=1, tiled=True)]
    all_to_all x1 -> x0, blocking collectives: 259 us -> none  [shards(): lax.all_to_all(outgoing.reshape(experts_all, capacity, features), ('node'...]
    unnamed x1 -> x0, blocking collectives: 176 us -> none
    psum x1 -> x0, blocking collectives: 162 us -> none  [shards(): lax.psum((counts, share_sums), ('dp', 'node', 'innode'))]
    pallas_call x0 -> x1, Pallas kernels: none -> 123 us  [shards(): pl.pallas_call(functools.partial(kernel, dims), out_shape=(jax.ShapeDtype...]
    dot_general x4 -> x0, matrix products: 10.5 us -> none  [the longest x1 5.57 us: apply_experts(): jnp.einsum('sekh,ehd->sekd', hidden, w_down, preferred_element_type=jnp.f...]
  transfers between devices with their start and end apart: 1 -> 0, of which waited for: 0 -> 0; matrix products, arithmetic and copies ran while one was open for 0% -> 0% of each run, Pallas kernels for 0% -> 0%
where the time goes in v2:
time: 127 us
  Pallas kernels  123 us (97%)
  between operations  2.39 us (2%)
  local copies, waits for them, and re-layouts  1.86 us (1%)
    pallas_call x1, Pallas kernels, shards(): pl.pallas_call(functools.partial(kernel, dims), out_shape=(jax.ShapeDtype...  123 us

profile of v2, /device:TPU:1, one launch (start us, length us, event | category | flops | bytes accessed | tf_op | source)
XLA Modules:
  0.0 127.0 jit_solution(11822234568094526475)
XLA Ops:
  0.6 122.7 %expert_layer.1 = (bf16[1,1,4096]{2,1,0:T(2,128)(2,1)}, f32[1,64]{1,0:T(1,128)}, f32[1,1]{1,0:T(1,128)}) custom-call(bf16[1,1,4096]{2,1,0:T(2,128)(2,1)} %tokens.1, s32[1,1,8]{2,1,0:T(1,128)} %routes.1, s32[1,1,8]{2,1,0:T(1,128)} %gate_num.1, bf16[1,4096,128]{2,1,0:T(8,128)(2,1)} %wg.1, bf16[1,4096,128]{2,1,0:T(8,128)(2,1)} %wu.1, bf16[1,128,4096]{2,1,0:T(8,128)(2,1)} %wd.1), custom_call_target="tpu_custom_call" | custom-call | tf_op jit(solution)/shard_map/expert_layer/pallas_call | solution.py:530
  123.4 0.0 copy-start
  123.4 1.3 %copy.12 = bf16[1,1,4096]{2,1,0:T(2,128)(2,1)} copy(bf16[1,1,4096]{2,1,0:T(2,128)(2,1)} %get-tuple-element.12) | data formatting | bytes 16384
  124.7 0.0 copy-done
  124.7 0.5 copy.13
Async XLA Ops:
  123.4 1.4 %copy-start = (f32[1,64]{1,0:T(1,128)S(1)}, f32[1,64]{1,0:T(1,128)}, u32[]{:S(2)}) copy-start(f32[1,64]{1,0:T(1,128)} %get-tuple-element.7) | copy-start | bytes 772

commit v3 on v2

--- a/solution.py
+++ b/solution.py
@@ -10,7 +10,7 @@
 GATE_DEN = 256
 MESH = pl.DeviceIdType.MESH
 SIDE = 4
-N_SEND, N_RECV = 33, 102
+N_SEND, N_RECV = 33, 98
 FAR = 4
 
 
@@ -100,8 +100,8 @@
     greet = [along(f) for f in far]
     greet += [along(o) for o in range(near // 2, 0, -1)] + [along(-o) for o in range(near // 2, 0, -1)]
     greet = greet if near > 2 else greet[:2] + [along(1), along(-1)]
-    greet += [device(z, core, py, side(px, o)) for o in (1, -1)]
-    greet += [device(z, core, side(py, o), px) for o in (1, -1)]
+    greet += [device(z, core, py, side(px, o)) for o in (2, 1, -1)]
+    greet += [device(z, core, side(py, o), px) for o in (2, 1, -1)]
     greet += [partner]
     for target in greet:
         pl.semaphore_signal(barrier, inc=1, device_id=target, device_id_type=MESH)
@@ -211,6 +211,8 @@
             for d in (1, -1):
                 src = block(xb, q, h, 0, 0)
                 send(("p1", q, h), src, src, xy_device(h, d, 0), None, ("full", q, h))
+
+    def ag_middle(q):
         for h in range(2):
             ag_second(q, h, 0)
 
@@ -225,8 +227,11 @@
             for d in (1, -1):
                 src = block(xb, q, h, -d, 0, low if d == 1 else high)
                 send(("p1f", q, h), src, src, xy_device(h, d, 0), None, ("half", q, h))
-            for d in (1, -1):
-                ag_second(q, h, -d)
+
+    def ag_sides(q):
+        for d in (1, -1):
+            for h in range(2):
+                ag_second(q, h, d)
 
     def ag_second_forward(q, a):
         for h in range(2):
@@ -256,13 +261,14 @@
     turn = (2, 1, -1, 0)
 
     def project(q):
+        rows = SIDE * SIDE * chunk
+        acc = jnp.dot(xb[q, 0].reshape(rows, part), w1[0], preferred_element_type=f32)
+        acc = acc + jnp.dot(xb[q, 1].reshape(rows, part), w1[1], preferred_element_type=f32)
+        ps[q] = acc[:, 2 * hid : 4 * hid].reshape(SIDE, SIDE * chunk, 2 * hid)
         for t in turn:
             yy = side(py, t)
-            acc = jnp.dot(xb[q, 0, yy].reshape(SIDE * chunk, part), w1[0], preferred_element_type=f32)
-            acc = acc + jnp.dot(xb[q, 1, yy].reshape(SIDE * chunk, part), w1[1], preferred_element_type=f32)
-            pa[q, yy] = acc[:, 0 : 2 * hid]
-            ps[q, yy] = acc[:, 2 * hid : 4 * hid]
             send(("ps", q, t), ps.at[q, yy], pr.at[q, yy], partner, None, ("ps", q))
+        pa[q] = acc[:, 0 : 2 * hid].reshape(SIDE, SIDE * chunk, 2 * hid)
 
     def activate(q):
         for t in turn:
@@ -381,30 +387,18 @@
         meta_t[...] = jnp.full_like(meta_t, -1.0)
         meta_t[pl.ds(0, 2 * chunk), :] = mz[:, 0, :]
         codes[py, px] = jnp.transpose(meta_t[...])[0 : 2 * per_token]
-        for o in (1, -1):
+        for o in (2, 1, -1):
             src = codes.at[py, px]
-            send(("mx", o), src, src, device(z, core, py, side(px, o)), None, "mx")
-
-    def codes_x():
-        arrived(("mx", 1), codes.at[0, 0])
-        src = codes.at[py, side(px, -1)]
-        send(("mx", 2), src, src, device(z, core, py, side(px, 1)), None, "mx")
+            send("mx", src, src, device(z, core, py, side(px, o)))
 
     def codes_row():
-        arrived(("mx", -1), codes.at[0, 0])
-        arrived(("mx", 2), codes.at[0, 0])
-        for o in (1, -1):
+        arrived("mx", codes.at[0, pl.ds(0, 3)])
+        for o in (2, 1, -1):
             src = codes.at[py]
-            send(("my", o), src, src, device(z, core, side(py, o), px), None, "my")
-
-    def codes_y():
-        arrived(("my", 1), codes.at[0])
-        src = codes.at[side(py, -1)]
-        send(("my", 2), src, src, device(z, core, side(py, 1), px), None, "my")
+            send("my", src, src, device(z, core, side(py, o), px))
 
     def gates():
-        arrived(("my", -1), codes.at[0])
-        arrived(("my", 2), codes.at[0])
+        arrived("my", codes.at[pl.ds(0, 3)])
         expert = (node * (SIDE * SIDE) + inn).astype(f32)
         meta_t[...] = jnp.zeros_like(meta_t)
         for yy in range(SIDE):
@@ -423,50 +417,51 @@
 
     spread_in(0)
     ag_own(0)
+    ag_middle(0)
     spread_in(1)
     ag_own(1)
     codes_own()
     ag_first_forward(0)
+    ag_sides(0)
+    ag_first_forward(1)
+    ag_middle(1)
+    ag_opposite(0)
+    ag_opposite(1)
     ag_second_forward(0, 0)
-    ag_opposite(0)
-    codes_x()
-    ag_first_forward(1)
     ag_second_forward(0, 1)
     ag_second_forward(0, -1)
+    ag_sides(1)
     codes_row()
+    ag_second_forward(0, 2)
     ag_second_forward(1, 0)
-    ag_opposite(1)
-    ag_second_forward(0, 2)
-    codes_y()
+    ag_second_forward(1, 2)
     pltpu.make_async_copy(w1.at[:, :, pl.ds(0, 2 * hid)], w1.at[:, :, pl.ds(0, 2 * hid)], lsem.at[3]).wait()
     pltpu.make_async_copy(w2.at[pl.ds(0, hid), :], w2.at[pl.ds(0, hid), :], lsem.at[4]).wait()
     arrived("w1", w1.at[:, :, pl.ds(2 * hid, 2 * hid)])
     arrived("w2", w2.at[pl.ds(hid, hid), :])
-    gates()
-
     ag_finish(0)
     project(0)
     ag_second_forward(1, 1)
     ag_second_forward(1, -1)
+    gates()
     activate(0)
-    ag_second_forward(1, 2)
     expand(0)
     ag_finish(1)
     project(1)
     rs_side(0, 2)
-    activate(1)
     rs_side(0, 1)
     rs_side(0, -1)
+    activate(1)
     rs_side(0, 0)
+    rs_second_far(0)
     expand(1)
-    rs_second_far(0)
     rs_second_side(0)
     rs_side(1, 2)
     rs_side(1, 1)
     rs_side(1, -1)
+    rs_second_far(1)
     rs_side(1, 0)
     rs_last(0)
-    rs_second_far(1)
     rs_second_side(1)
     rs_last(1)
 

time: 127 us -> 122 us (0.961)
  Pallas kernels: 123 us -> 117 us
    pallas_call x1, Pallas kernels: 123 us -> 117 us  [shards(): pl.pallas_call(functools.partial(kernel, dims), out_shape=(jax.ShapeDtype...]
where the time goes in v3:
time: 122 us; the launch traced here: 121 us
  Pallas kernels  117 us (96%)
  between operations  2.39 us (2%)
  local copies, waits for them, and re-layouts  1.86 us (2%)
    pallas_call x1, Pallas kernels, shards(): pl.pallas_call(functools.partial(kernel, dims), out_shape=(jax.ShapeDtype...  117 us

profile of v3, /device:TPU:1, one launch (start us, length us, event | category | flops | bytes accessed | tf_op | source)
XLA Modules:
  0.0 121.4 jit_solution(10533061713961408024)
XLA Ops:
  0.6 117.2 %expert_layer.1 = (bf16[1,1,4096]{2,1,0:T(2,128)(2,1)}, f32[1,64]{1,0:T(1,128)}, f32[1,1]{1,0:T(1,128)}) custom-call(bf16[1,1,4096]{2,1,0:T(2,128)(2,1)} %tokens.1, s32[1,1,8]{2,1,0:T(1,128)} %routes.1, s32[1,1,8]{2,1,0:T(1,128)} %gate_num.1, bf16[1,4096,128]{2,1,0:T(8,128)(2,1)} %wg.1, bf16[1,4096,128]{2,1,0:T(8,128)(2,1)} %wu.1, bf16[1,128,4096]{2,1,0:T(8,128)(2,1)} %wd.1), custom_call_target="tpu_custom_call" | custom-call | tf_op jit(solution)/shard_map/expert_layer/pallas_call | solution.py:525
  117.8 0.0 copy-start
  117.8 1.3 %copy.12 = bf16[1,1,4096]{2,1,0:T(2,128)(2,1)} copy(bf16[1,1,4096]{2,1,0:T(2,128)(2,1)} %get-tuple-element.12) | data formatting | bytes 16384
  119.2 0.0 copy-done
  119.2 0.5 copy.13
Async XLA Ops:
  117.8 1.4 %copy-start = (f32[1,64]{1,0:T(1,128)S(1)}, f32[1,64]{1,0:T(1,128)}, u32[]{:S(2)}) copy-start(f32[1,64]{1,0:T(1,128)} %get-tuple-element.7) | copy-start | bytes 772

commit v4 on v3

--- a/solution.py
+++ b/solution.py
@@ -187,7 +187,7 @@
 
     near_rest = pl.ds(members, (near - 1) * members)
     arrived("far", x3.at[pl.ds(0, members)])
-    for g in range(1, near):
+    for g in [*range(1, per_chunk), *range(near - 1, per_chunk - 1, -1)]:
         send("near", x3.at[pl.ds(0, members)], x3.at[pl.ds(g * members, members)], along(steps[g]), ("near", g // per_chunk))
     arrived("farm", mz.at[pl.ds(0, members)])
     for g in range(1, near):
@@ -353,7 +353,7 @@
             for i in range(per):
                 spread[:, h * per + i, :] = total[:, i * 128 : (i + 1) * 128]
         y3[q] = spread[...].astype(bf16)
-        for g in range(q * per_chunk, (q + 1) * per_chunk):
+        for g in reversed(range(q * per_chunk, (q + 1) * per_chunk)):
             if g:
                 src = y3.at[q, pl.ds((g - q * per_chunk) * members, members)]
                 send("zn", src, rn.at[g - 1], along(-steps[g]))

time: 122 us -> 122 us (level)
  no operation moved by 1% of the time
where the time goes in v4:
time: 122 us
  Pallas kernels  117 us (96%)
  between operations  2.39 us (2%)
  local copies, waits for them, and re-layouts  1.86 us (2%)
    pallas_call x1, Pallas kernels, shards(): pl.pallas_call(functools.partial(kernel, dims), out_shape=(jax.ShapeDtype...  117 us

profile of v4, /device:TPU:1, one launch (start us, length us, event | category | flops | bytes accessed | tf_op | source)
XLA Modules:
  0.0 121.7 jit_solution(6482724927840572669)
XLA Ops:
  0.6 117.5 %expert_layer.1 = (bf16[1,1,4096]{2,1,0:T(2,128)(2,1)}, f32[1,64]{1,0:T(1,128)}, f32[1,1]{1,0:T(1,128)}) custom-call(bf16[1,1,4096]{2,1,0:T(2,128)(2,1)} %tokens.1, s32[1,1,8]{2,1,0:T(1,128)} %routes.1, s32[1,1,8]{2,1,0:T(1,128)} %gate_num.1, bf16[1,4096,128]{2,1,0:T(8,128)(2,1)} %wg.1, bf16[1,4096,128]{2,1,0:T(8,128)(2,1)} %wu.1, bf16[1,128,4096]{2,1,0:T(8,128)(2,1)} %wd.1), custom_call_target="tpu_custom_call" | custom-call | tf_op jit(solution)/shard_map/expert_layer/pallas_call | solution.py:525
  118.1 0.0 copy-start
  118.1 1.3 %copy.12 = bf16[1,1,4096]{2,1,0:T(2,128)(2,1)} copy(bf16[1,1,4096]{2,1,0:T(2,128)(2,1)} %get-tuple-element.12) | data formatting | bytes 16384
  119.5 0.0 copy-done
  119.5 0.5 copy.13
Async XLA Ops:
  118.1 1.4 %copy-start = (f32[1,64]{1,0:T(1,128)S(1)}, f32[1,64]{1,0:T(1,128)}, u32[]{:S(2)}) copy-start(f32[1,64]{1,0:T(1,128)} %get-tuple-element.7) | copy-start | bytes 772
